TPU v7x, 32 devices: a whole 2x2x4 slice. The times are simulated.
32 devices in a mesh: bead: 2 (over y), atom: 4 (over z), ka: 4 (over x, core).
Axes of the slice: x: 2, y: 2, z: 4, core: 2. Of those that a mesh axis runs over, the one named last changes fastest.
Arguments:
- frac: float32 [3, 8192], P(None, ('bead', 'atom')), parts along dimension 1, may hold values from 0 to 1
- feat: bfloat16 [8192, 64], P(('bead', 'atom')), parts along dimension 0, may hold values from -6 to 6
- cotan: bfloat16 [8192, 64], P(('bead', 'atom')), parts along dimension 0, may hold values from -0.059814453 to 0.059814453
- kidx: int32 [3, 8192], P(None, 'ka'), may hold values from -12 to 12
- smear: float32 [64], replicated, may hold values from 0.001 to 0.01
Outputs:
- messages: float32 [8192, 64], P(('bead', 'atom')), parts along dimension 0
- forces: float32 [3, 8192], P(None, ('bead', 'atom')), parts along dimension 1
There are 2 independent parts, one for each index of `bead`. A program takes and returns all parts, laid end to end along the dimension named above; an argument that names none is the same for every part. Nothing has to cross between parts.
All inputs are finite; a program needn't handle non-finite values.
Results may differ from a plain program's by a relative error of at most 0.0075.
Values may be sent and summed in bfloat16 or wider, within the bound.
A program may use at most 64 MiB of HBM per device.

v0:
```python
import functools
import math

import jax
import jax.numpy as jnp
import numpy as np
from jax import lax
from jax.experimental import pallas as pl
from jax.experimental.pallas import tpu as pltpu
from jax.sharding import PartitionSpec as P

TWO_PI = 2.0 * math.pi
MESH = pl.DeviceIdType.MESH
F32 = jnp.float32
BF16 = jnp.bfloat16
ROUND = 1.5 * 2.0**23


def half_turn_fit():
    nodes = 0.125 * (1.0 - np.cos(np.pi * (np.arange(400) + 0.5) / 400))
    t = np.sqrt(nodes)
    root = math.sqrt(2.0)
    sin_c = np.polynomial.chebyshev.Chebyshev.fit(nodes, root * np.sin(np.pi * t) / t, 3, domain=[0, 0.25])
    cos_c = np.polynomial.chebyshev.Chebyshev.fit(nodes, root * np.cos(np.pi * t), 3, domain=[0, 0.25])
    to_list = lambda fit: [float(v) for v in fit.convert(kind=np.polynomial.Polynomial, domain=[-1, 1]).coef]
    return to_list(sin_c), to_list(cos_c)


SIN_C, COS_C = half_turn_fit()


def turn(spot):
    t = spot - ((spot + ROUND) - ROUND)
    u = t * t
    half_s = t * (((SIN_C[3] * u + SIN_C[2]) * u + SIN_C[1]) * u + SIN_C[0])
    half_c = ((COS_C[3] * u + COS_C[2]) * u + COS_C[1]) * u + COS_C[0]
    return (1.0 - half_s * half_s).astype(BF16), (half_s * half_c).astype(BF16)


def kernel(
    atoms, frac_ref, feat_ref, cot_ref, kidx_ref, smear_ref, msg_ref, force_ref,
    fr, fs, xt, ph, gt, part, rc, s1, rx, s2, rz, fin,
    fsend, frecv, zsend, zrecv, xsend, xrecv, csend, crecv,
    pcs, pcr, pxs, pxr, pzs, pzr, ags, agr,
):
    bead = lax.axis_index("bead")
    z = lax.axis_index("atom")
    ka = lax.axis_index("ka")
    x = ka // 2
    core = lax.rem(ka, 2)
    slot = core * 2 + x
    other_core = 1 - core
    dev_z = [(bead, lax.rem(z + j, 4), ka) for j in range(4)]
    dev_core = (bead, z, x * 2 + other_core)
    dev_x = (bead, z, (1 - x) * 2 + core)
    dev_diag = (bead, z, (1 - x) * 2 + other_core)
    kn = kidx_ref.shape[1] // 4
    quarter = fr.shape[2] // 4

    barrier = pltpu.get_barrier_semaphore()
    for dev in dev_z[1:] + [dev_core, dev_x, dev_diag]:
        pl.semaphore_signal(barrier, inc=1, device_id=dev, device_id_type=MESH)

    def remote(src, dst, send, recv, dev):
        return pltpu.make_async_remote_copy(
            src_ref=src, dst_ref=dst, send_sem=send, recv_sem=recv, device_id=dev, device_id_type=MESH
        )

    fr[0] = jnp.zeros(fr.shape[1:], F32)
    fr[0, 0:3, :] = frac_ref[...]
    for s in range(4):
        rows = pl.ds(s * quarter, quarter)
        both = jnp.concatenate([feat_ref[rows, :].astype(F32), cot_ref[rows, :].astype(F32)], axis=1)
        xt[0, s] = both.T.astype(BF16)

    pl.semaphore_wait(barrier, 6)
    fcopies = [remote(fr.at[0], fr.at[4 - j], fsend.at[j], frecv.at[4 - j], dev_z[j]) for j in (1, 3, 2)]
    for c in fcopies:
        c.start()
    zcopies = [
        remote(xt.at[0, slot], xt.at[4 - j, slot], zsend.at[j], zrecv.at[4 - j], dev_z[j]) for j in (1, 3, 2)
    ]
    for c in zcopies:
        c.start()

    kf = kidx_ref[:, pl.ds(pl.multiple_of(z * kn, 128), kn)].astype(F32)
    k0, k1, k2 = kf[0:1], kf[1:2], kf[2:3]
    row = lax.broadcasted_iota(jnp.int32, (8, kn), 0)
    k8 = jnp.where(row == 0, k0, jnp.where(row == 1, k1, jnp.where(row == 2, k2, 0.0)))
    kt = jnp.concatenate([k8, k8, k8, jnp.zeros((104, kn), F32)], axis=0).T.astype(BF16)[:, :32]

    def phases(r):
        f = fr[r]
        hi = f.astype(BF16).astype(F32)
        mid = (f - hi).astype(BF16).astype(F32)
        lo = f - hi - mid
        fs[...] = jnp.concatenate([hi, mid, lo, jnp.zeros_like(f)], axis=0).astype(BF16)
        for s in range(4):
            spot = jnp.dot(kt, fs[:, s * quarter : (s + 1) * quarter], preferred_element_type=F32)
            c, sn = turn(spot)
            ph[r, s, 0:kn, :] = c
            ph[r, s, kn : 2 * kn, :] = sn

    def sums_of(r):
        total = None
        for s in range(4):
            term = lax.dot_general(
                ph[r, s], xt[r, s], (((1,), (1,)), ((), ())), preferred_element_type=F32
            )
            total = term if total is None else total + term
        return total

    def wait_frac(r):
        remote(fr.at[0], fr.at[r], fsend.at[0], frecv.at[r], dev_x).wait_recv()

    phases(0)
    xcopies = []
    for r in (1, 3, 2):
        remote(xt.at[0, slot], xt.at[r, slot], zsend.at[0], zrecv.at[r], dev_x).wait_recv()
        c = remote(xt.at[r, slot], xt.at[r, slot], xsend.at[r], xrecv.at[r], dev_x)
        c.start()
        xcopies.append(c)
    wait_frac(1)
    phases(1)
    ccopies = []
    mate = core * 2 + (1 - x)
    two = pl.ds(core * 2, 2)
    for r in (1, 3, 2):
        remote(xt.at[r, mate], xt.at[r, mate], xsend.at[r], xrecv.at[r], dev_x).wait_recv()
        c = remote(xt.at[r, two], xt.at[r, two], csend.at[r], crecv.at[r], dev_core)
        c.start()
        ccopies.append(c)
    wait_frac(3)
    phases(3)
    wait_frac(2)
    phases(2)

    total = sums_of(0)
    other_two = pl.ds(other_core * 2, 2)
    for r in (1, 3, 2):
        remote(xt.at[r, other_two], xt.at[r, other_two], csend.at[r], crecv.at[r], dev_core).wait_recv()
        total = total + sums_of(r)
    sums_t = total.T

    nsq = k0 * k0 + k1 * k1 + k2 * k2
    srow = jnp.concatenate([smear_ref[...], smear_ref[...]], axis=1)
    scol = jnp.broadcast_to(srow, (128, 128)).T
    scol = jnp.concatenate([scol] * (kn // 128), axis=1)
    weights = jnp.exp(-scol * nsq) / (1.0 + nsq) * atoms ** (-0.5)
    wc = (sums_t[:, :kn] * weights).astype(BF16)
    ws = (sums_t[:, kn:] * weights).astype(BF16)
    half = wc.shape[0] // 2
    gt[384:448, 0:kn] = wc[:half]
    gt[384:448, kn : 2 * kn] = ws[:half]
    wc, ws = wc.astype(F32), ws.astype(F32)
    wc = jnp.concatenate([wc[half:], wc[:half]], axis=0)
    ws = jnp.concatenate([ws[half:], ws[:half]], axis=0)
    for d, kd in enumerate((k0, k1, k2)):
        gt[128 * d : 128 * d + 128, 0:kn] = (ws * kd).astype(BF16)
        gt[128 * d : 128 * d + 128, kn : 2 * kn] = (wc * -kd).astype(BF16)

    frow = lax.broadcasted_iota(jnp.int32, (16, quarter), 0)

    def outputs_of(r, i):
        for s in range(4):
            out = jnp.dot(gt[...], ph[r, s], preferred_element_type=F32)
            pair = xt[r, s].astype(F32)
            f = [
                -TWO_PI * jnp.sum(out[128 * d : 128 * d + 128] * pair, axis=0, keepdims=True) for d in range(3)
            ]
            part[i, s, 0:64, :] = out[384:448].astype(BF16)
            part[i, s, 64:80, :] = jnp.where(
                frow == 0, f[0], jnp.where(frow == 1, f[1], jnp.where(frow == 2, f[2], 0.0))
            ).astype(BF16)

    pending = []

    def begin(c):
        c.start()
        pending.append(c)

    own = None
    for i in range(6):
        if i < 4:
            outputs_of((1 + i) % 4, i)
            begin(remote(part.at[i, other_two], rc.at[i], pcs.at[i], pcr.at[i], dev_core))
        if 1 <= i < 5:
            j = i - 1
            remote(part.at[j, two], rc.at[j], pcs.at[j], pcr.at[j], dev_core).wait_recv()
            s1[j] = (part[j, two].astype(F32) + rc[j].astype(F32)).astype(BF16)
            begin(remote(s1.at[j, 1 - x], rx.at[j], pxs.at[j], pxr.at[j], dev_x))
        if i >= 2:
            j = i - 2
            remote(s1.at[j, x], rx.at[j], pxs.at[j], pxr.at[j], dev_x).wait_recv()
            value = s1[j, x].astype(F32) + rx[j].astype(F32)
            if j < 3:
                s2[j] = value.astype(BF16)
                begin(remote(s2.at[j], rz.at[j], pzs.at[j], pzr.at[j], dev_z[1 + j]))
            else:
                own = value
    for j in range(3):
        remote(s2.at[j], rz.at[j], pzs.at[j], pzr.at[j], dev_x).wait_recv()
        own = own + rz[j].astype(F32)
    fin[slot] = own.astype(BF16)
    for j, dev in enumerate((dev_x, dev_core, dev_diag)):
        begin(remote(fin.at[slot], fin.at[slot], ags.at[j], agr.at[j], dev))
    slots = (mate, other_core * 2 + x, other_core * 2 + (1 - x))
    for j, dev in enumerate((dev_x, dev_core, dev_diag)):
        remote(fin.at[slots[j]], fin.at[slots[j]], ags.at[j], agr.at[j], dev).wait_recv()
    for s in range(4):
        msg_ref[s * quarter : (s + 1) * quarter, :] = fin[s, 0:64, :].astype(F32).T
        force_ref[:, s * quarter : (s + 1) * quarter] = fin[s, 64:80, :].astype(F32)[0:3]
    for c in fcopies + zcopies + xcopies + ccopies + pending:
        c.wait_send()


def fast_on_device(frac, feat, cotan, kidx, smear):
    rows, chans = feat.shape
    kn = kidx.shape[1] // 4
    quarter = rows // 4
    dma = pltpu.SemaphoreType.DMA
    vmem = pl.BlockSpec(memory_space=pltpu.VMEM)
    return pl.pallas_call(
        functools.partial(kernel, 4 * rows),
        out_shape=(jax.ShapeDtypeStruct((rows, chans), F32), jax.ShapeDtypeStruct((3, rows), F32)),
        in_specs=[vmem] * 5,
        out_specs=(vmem, vmem),
        scratch_shapes=[
            pltpu.VMEM((4, 8, rows), F32),
            pltpu.VMEM((32, rows), BF16),
            pltpu.VMEM((4, 4, 128, quarter), BF16),
            pltpu.VMEM((4, 4, 2 * kn, quarter), BF16),
            pltpu.VMEM((448, 2 * kn), BF16),
            pltpu.VMEM((4, 4, 80, quarter), BF16),
            pltpu.VMEM((4, 2, 80, quarter), BF16),
            pltpu.VMEM((4, 2, 80, quarter), BF16),
            pltpu.VMEM((4, 80, quarter), BF16),
            pltpu.VMEM((3, 80, quarter), BF16),
            pltpu.VMEM((3, 80, quarter), BF16),
            pltpu.VMEM((4, 80, quarter), BF16),
        ]
        + [dma((4,))] * 16,
        compiler_params=pltpu.CompilerParams(
            collective_id=0, has_side_effects=True, vmem_limit_bytes=48 * 1024 * 1024
        ),
    )(frac, feat, cotan, kidx, smear.reshape(1, chans))


def over_rows(table, columns):
    return lax.dot_general(table, columns, (((0,), (0,)), ((), ())), preferred_element_type=F32)


def plain_on_device(frac, feat, cotan, kidx, smear):
    rows, chans = feat.shape
    atoms = rows * lax.axis_size("atom")
    nf = kidx.astype(F32)
    nsq = nf[0] * nf[0] + nf[1] * nf[1] + nf[2] * nf[2]
    weights = jnp.exp(-smear[None, :] * nsq[:, None]) / (1.0 + nsq)[:, None] * atoms ** (-0.5)
    spot = frac[0][:, None] * nf[0][None, :] + frac[1][:, None] * nf[1][None, :]
    cos_t, sin_t = turn(spot + frac[2][:, None] * nf[2][None, :])
    both = jnp.concatenate([feat, cotan], axis=1)
    sums = jnp.concatenate([over_rows(cos_t, both), over_rows(sin_t, both)], axis=1)
    total = lax.psum(sums, "atom")
    weighted = (total * jnp.tile(weights, (1, 4))).astype(BF16)
    left_c, left_s = weighted[:, : 2 * chans], weighted[:, 2 * chans :]
    msg = jnp.dot(cos_t, left_c[:, :chans], preferred_element_type=F32)
    msg = msg + jnp.dot(sin_t, left_s[:, :chans], preferred_element_type=F32)
    pair = jnp.concatenate([cotan, feat], axis=1)
    against = lambda a, b: lax.dot_general(a, b, (((1,), (1,)), ((), ())), preferred_element_type=F32)
    p_part, q_part = against(pair, left_c), against(pair, left_s)
    slope = (cos_t.astype(F32) * q_part - sin_t.astype(F32) * p_part).astype(BF16)
    force = -TWO_PI * against(kidx.astype(BF16), slope)
    return lax.psum(msg, "ka"), lax.psum(force, "ka")


def on_device(frac, feat, cotan, kidx, smear):
    rows, chans = feat.shape
    fits = lax.axis_size("atom") == 4 and lax.axis_size("ka") == 4 and chans == 64
    fits = fits and rows % 512 == 0 and rows <= 1024 and kidx.shape[1] % 512 == 0 and kidx.shape[1] <= 2048
    return (fast_on_device if fits else plain_on_device)(frac, feat, cotan, kidx, smear)


def solution(mesh):
    return jax.shard_map(
        on_device,
        mesh=mesh,
        in_specs=(
            P(None, ("bead", "atom")),
            P(("bead", "atom"), None),
            P(("bead", "atom"), None),
            P(None, "ka"),
            P(),
        ),
        out_specs=(P(("bead", "atom"), None), P(None, ("bead", "atom"))),
        check_vma=False,
    )
```

profile of v0, /device:TPU:0, one launch (start us, length us, event | category | flops | bytes accessed | tf_op | source)
XLA Modules:
  0.0 48.0 jit_solution(9742732653934929942)
XLA Ops:
  0.6 0.0 copy-start.3
  0.6 1.1 %copy.7.feat_ref = bf16[1024,64]{1,0:T(8,128)(2,1)S(1)} copy(bf16[1024,64]{0,1:T(8,128)(2,1)} %param.6) | data formatting | bytes 262144 | tf_op args[1]
  1.8 0.0 copy-done.3
  1.8 0.0 copy-start
  1.8 0.0 copy-start.1
  1.8 0.0 copy-start.2
  1.8 0.2 copy.8.cot_ref
  2.0 0.6 %copy-done = s32[3,2048]{1,0:T(4,128)S(1)} copy-done((s32[3,2048]{1,0:T(4,128)S(1)}, s32[3,2048]{1,0:T(4,128)}, u32[]{:S(2)}) %copy-start) | copy-done | bytes 24600
  2.5 0.0 copy-done.1
  2.5 0.0 copy-done.2
  2.5 44.0 %shard_map.68 = (f32[1024,64]{1,0:T(8,128)S(1)}, f32[3,1024]{1,0:T(4,128)S(1)}) custom-call(f32[3,1024]{1,0:T(4,128)S(1)} %copy-done.1, bf16[1024,64]{1,0:T(8,128)(2,1)S(1)} %copy.7.feat_ref, bf16[1024,64]{1,0:T(8,128)(2,1)S(1)} %copy.8.cot_ref, s32[3,2048]{1,0:T(4,128)S(1)} %copy-done, f32[1,64]{1,0:T(1,128)S(1)} %bitcast.1), custom_call_target="tpu_custom_call" | custom-call | tf_op jit(solution)/shard_map/pallas_call | solution.py:223
  46.5 0.9 %copy.9 = f32[1024,64]{0,1:T(8,128)} copy(f32[1024,64]{1,0:T(8,128)S(1)} %get-tuple-element.2) | data formatting | bytes 524288 | tf_op jit(solution)/shard_map/pallas_call | solution.py:223
  47.4 0.6 %copy.11 = f32[3,1024]{1,0:T(4,128)} copy(f32[3,1024]{1,0:T(4,128)S(1)} %get-tuple-element.7) | data formatting | bytes 24576
Async XLA Ops:
  0.6 1.1 %copy-start.3 = (bf16[1024,64]{0,1:T(8,128)(2,1)S(1)}, bf16[1024,64]{0,1:T(8,128)(2,1)}, u32[]{:S(2)}) copy-start(bf16[1024,64]{0,1:T(8,128)(2,1)} %param.7) | copy-start | bytes 393220
  1.8 0.8 %copy-start = (s32[3,2048]{1,0:T(4,128)S(1)}, s32[3,2048]{1,0:T(4,128)}, u32[]{:S(2)}) copy-start(s32[3,2048]{1,0:T(4,128)} %kidx_ref.1) | copy-start | bytes 73732
  1.8 0.8 %copy-start.1 = (f32[3,1024]{1,0:T(4,128)S(1)}, f32[3,1024]{1,0:T(4,128)}, u32[]{:S(2)}) copy-start(f32[3,1024]{1,0:T(4,128)} %frac_ref.1) | copy-start | bytes 36868
  1.8 0.7 %copy-start.2 = (f32[64]{0:T(128)S(1)}, f32[64]{0:T(128)}, u32[]{:S(2)}) copy-start(f32[64]{0:T(128)} %param.9) | copy-start | bytes 772
where the time goes:
time: 48.2 us; the launch traced here: 48 us
  Pallas kernels  44 us (91%)
  local copies, waits for them, and re-layouts  3.34 us (7%)
  between operations  0.69 us (1%)
    pallas_call x1, Pallas kernels, fast_on_device(): pl.pallas_call(functools.partial(kernel, 4 * rows), out_shape=(jax.ShapeD...  44 us
    unnamed x11, local copies, waits for them, and re-layouts  2.45 us

commit v1 on v0

--- a/solution.py
+++ b/solution.py
@@ -38,8 +38,9 @@
 
 
 def kernel(
-    atoms, frac_ref, feat_ref, cot_ref, kidx_ref, smear_ref, msg_ref, force_ref,
-    fr, fs, xt, ph, gt, part, rc, s1, rx, s2, rz, fin,
+    atoms, frac_hbm, feat_hbm, cot_hbm, kidx_hbm, smear_hbm, msg_ref, force_ref,
+    frac_ref, feat_ref, cot_ref, kidx_ref, smear_ref, lsem,
+    fr, f8, fs, xt, ph, gt, part, rc, s1, rx, s2, rz, fin,
     fsend, frecv, zsend, zrecv, xsend, xrecv, csend, crecv,
     pcs, pcr, pxs, pxr, pzs, pzr, ags, agr,
 ):
@@ -54,7 +55,7 @@
     dev_core = (bead, z, x * 2 + other_core)
     dev_x = (bead, z, (1 - x) * 2 + core)
     dev_diag = (bead, z, (1 - x) * 2 + other_core)
-    kn = kidx_ref.shape[1] // 4
+    kn = kidx_ref.shape[1]
     quarter = fr.shape[2] // 4
 
     barrier = pltpu.get_barrier_semaphore()
@@ -66,12 +67,24 @@
             src_ref=src, dst_ref=dst, send_sem=send, recv_sem=recv, device_id=dev, device_id_type=MESH
         )
 
-    fr[0] = jnp.zeros(fr.shape[1:], F32)
-    fr[0, 0:3, :] = frac_ref[...]
+    loads = [
+        pltpu.make_async_copy(frac_hbm, frac_ref, lsem.at[0]),
+        pltpu.make_async_copy(feat_hbm, feat_ref, lsem.at[1]),
+        pltpu.make_async_copy(cot_hbm, cot_ref, lsem.at[2]),
+        pltpu.make_async_copy(kidx_hbm.at[:, pl.ds(pl.multiple_of(z * kn, 128), kn)], kidx_ref, lsem.at[3]),
+        pltpu.make_async_copy(smear_hbm, smear_ref, lsem.at[4]),
+    ]
+    for c in loads:
+        c.start()
+    f8[...] = jnp.zeros(f8.shape, F32)
+    loads[0].wait()
+    fr[0] = frac_ref[...]
+    loads[1].wait()
+    loads[2].wait()
     for s in range(4):
-        rows = pl.ds(s * quarter, quarter)
-        both = jnp.concatenate([feat_ref[rows, :].astype(F32), cot_ref[rows, :].astype(F32)], axis=1)
-        xt[0, s] = both.T.astype(BF16)
+        cols = pl.ds(s * quarter, quarter)
+        xt[0, s, 0:64, :] = feat_ref[:, cols]
+        xt[0, s, 64:128, :] = cot_ref[:, cols]
 
     pl.semaphore_wait(barrier, 6)
     fcopies = [remote(fr.at[0], fr.at[4 - j], fsend.at[j], frecv.at[4 - j], dev_z[j]) for j in (1, 3, 2)]
@@ -83,14 +96,17 @@
     for c in zcopies:
         c.start()
 
-    kf = kidx_ref[:, pl.ds(pl.multiple_of(z * kn, 128), kn)].astype(F32)
+    loads[3].wait()
+    loads[4].wait()
+    kf = kidx_ref[...].astype(F32)
     k0, k1, k2 = kf[0:1], kf[1:2], kf[2:3]
     row = lax.broadcasted_iota(jnp.int32, (8, kn), 0)
     k8 = jnp.where(row == 0, k0, jnp.where(row == 1, k1, jnp.where(row == 2, k2, 0.0)))
     kt = jnp.concatenate([k8, k8, k8, jnp.zeros((104, kn), F32)], axis=0).T.astype(BF16)[:, :32]
 
     def phases(r):
-        f = fr[r]
+        f8[0:3, :] = fr[r]
+        f = f8[...]
         hi = f.astype(BF16).astype(F32)
         mid = (f - hi).astype(BF16).astype(F32)
         lo = f - hi - mid
@@ -113,40 +129,51 @@
     def wait_frac(r):
         remote(fr.at[0], fr.at[r], fsend.at[0], frecv.at[r], dev_x).wait_recv()
 
-    phases(0)
-    xcopies = []
-    for r in (1, 3, 2):
-        remote(xt.at[0, slot], xt.at[r, slot], zsend.at[0], zrecv.at[r], dev_x).wait_recv()
-        c = remote(xt.at[r, slot], xt.at[r, slot], xsend.at[r], xrecv.at[r], dev_x)
-        c.start()
-        xcopies.append(c)
-    wait_frac(1)
-    phases(1)
-    ccopies = []
-    mate = core * 2 + (1 - x)
-    two = pl.ds(core * 2, 2)
-    for r in (1, 3, 2):
-        remote(xt.at[r, mate], xt.at[r, mate], xsend.at[r], xrecv.at[r], dev_x).wait_recv()
-        c = remote(xt.at[r, two], xt.at[r, two], csend.at[r], crecv.at[r], dev_core)
-        c.start()
-        ccopies.append(c)
-    wait_frac(3)
-    phases(3)
-    wait_frac(2)
-    phases(2)
-
-    total = sums_of(0)
-    other_two = pl.ds(other_core * 2, 2)
-    for r in (1, 3, 2):
-        remote(xt.at[r, other_two], xt.at[r, other_two], csend.at[r], crecv.at[r], dev_core).wait_recv()
-        total = total + sums_of(r)
-    sums_t = total.T
-
     nsq = k0 * k0 + k1 * k1 + k2 * k2
     srow = jnp.concatenate([smear_ref[...], smear_ref[...]], axis=1)
     scol = jnp.broadcast_to(srow, (128, 128)).T
     scol = jnp.concatenate([scol] * (kn // 128), axis=1)
     weights = jnp.exp(-scol * nsq) / (1.0 + nsq) * atoms ** (-0.5)
+    mate = core * 2 + (1 - x)
+    two = pl.ds(core * 2, 2)
+    other_two = pl.ds(other_core * 2, 2)
+    xcopies, ccopies = [], []
+
+    def forward_x(r):
+        remote(xt.at[0, slot], xt.at[r, slot], zsend.at[0], zrecv.at[r], dev_x).wait_recv()
+        xcopies.append(remote(xt.at[r, slot], xt.at[r, slot], xsend.at[r], xrecv.at[r], dev_x))
+        xcopies[-1].start()
+
+    def forward_core(r):
+        remote(xt.at[r, mate], xt.at[r, mate], xsend.at[r], xrecv.at[r], dev_x).wait_recv()
+        ccopies.append(remote(xt.at[r, two], xt.at[r, two], csend.at[r], crecv.at[r], dev_core))
+        ccopies[-1].start()
+
+    def wait_core(r):
+        remote(xt.at[r, other_two], xt.at[r, other_two], csend.at[r], crecv.at[r], dev_core).wait_recv()
+
+    phases(0)
+    wait_frac(1)
+    phases(1)
+    forward_x(1)
+    forward_x(3)
+    total = sums_of(0)
+    forward_core(1)
+    forward_x(2)
+    wait_frac(3)
+    phases(3)
+    forward_core(3)
+    wait_core(1)
+    total = total + sums_of(1)
+    forward_core(2)
+    wait_frac(2)
+    phases(2)
+    wait_core(3)
+    total = total + sums_of(3)
+    wait_core(2)
+    total = total + sums_of(2)
+    sums_t = total.T
+
     wc = (sums_t[:, :kn] * weights).astype(BF16)
     ws = (sums_t[:, kn:] * weights).astype(BF16)
     half = wc.shape[0] // 2
@@ -161,8 +188,8 @@
 
     frow = lax.broadcasted_iota(jnp.int32, (16, quarter), 0)
 
-    def outputs_of(r, i):
-        for s in range(4):
+    def outputs_of(r, i, slots):
+        for s in slots:
             out = jnp.dot(gt[...], ph[r, s], preferred_element_type=F32)
             pair = xt[r, s].astype(F32)
             f = [
@@ -179,25 +206,22 @@
         c.start()
         pending.append(c)
 
+    for i in range(4):
+        outputs_of((1 + i) % 4, i, (other_core * 2, other_core * 2 + 1))
+        begin(remote(part.at[i, other_two], rc.at[i], pcs.at[i], pcr.at[i], dev_core))
+    for i in range(4):
+        outputs_of((1 + i) % 4, i, (mate,))
+        remote(part.at[i, two], rc.at[i], pcs.at[i], pcr.at[i], dev_core).wait_recv()
+        s1[i] = (part[i, mate].astype(F32) + rc[i, 1 - x].astype(F32)).astype(BF16)
+        begin(remote(s1.at[i], rx.at[i], pxs.at[i], pxr.at[i], dev_x))
     own = None
-    for i in range(6):
-        if i < 4:
-            outputs_of((1 + i) % 4, i)
-            begin(remote(part.at[i, other_two], rc.at[i], pcs.at[i], pcr.at[i], dev_core))
-        if 1 <= i < 5:
-            j = i - 1
-            remote(part.at[j, two], rc.at[j], pcs.at[j], pcr.at[j], dev_core).wait_recv()
-            s1[j] = (part[j, two].astype(F32) + rc[j].astype(F32)).astype(BF16)
-            begin(remote(s1.at[j, 1 - x], rx.at[j], pxs.at[j], pxr.at[j], dev_x))
-        if i >= 2:
-            j = i - 2
-            remote(s1.at[j, x], rx.at[j], pxs.at[j], pxr.at[j], dev_x).wait_recv()
-            value = s1[j, x].astype(F32) + rx[j].astype(F32)
-            if j < 3:
-                s2[j] = value.astype(BF16)
-                begin(remote(s2.at[j], rz.at[j], pzs.at[j], pzr.at[j], dev_z[1 + j]))
-            else:
-                own = value
+    for i in range(4):
+        outputs_of((1 + i) % 4, i, (slot,))
+        remote(s1.at[i], rx.at[i], pxs.at[i], pxr.at[i], dev_x).wait_recv()
+        own = part[i, slot].astype(F32) + rc[i, x].astype(F32) + rx[i].astype(F32)
+        if i < 3:
+            s2[i] = own.astype(BF16)
+            begin(remote(s2.at[i], rz.at[i], pzs.at[i], pzr.at[i], dev_z[1 + i]))
     for j in range(3):
         remote(s2.at[j], rz.at[j], pzs.at[j], pzr.at[j], dev_x).wait_recv()
         own = own + rz[j].astype(F32)
@@ -208,7 +232,7 @@
     for j, dev in enumerate((dev_x, dev_core, dev_diag)):
         remote(fin.at[slots[j]], fin.at[slots[j]], ags.at[j], agr.at[j], dev).wait_recv()
     for s in range(4):
-        msg_ref[s * quarter : (s + 1) * quarter, :] = fin[s, 0:64, :].astype(F32).T
+        msg_ref[:, s * quarter : (s + 1) * quarter] = fin[s, 0:64, :].astype(F32)
         force_ref[:, s * quarter : (s + 1) * quarter] = fin[s, 64:80, :].astype(F32)[0:3]
     for c in fcopies + zcopies + xcopies + ccopies + pending:
         c.wait_send()
@@ -220,20 +244,27 @@
     quarter = rows // 4
     dma = pltpu.SemaphoreType.DMA
     vmem = pl.BlockSpec(memory_space=pltpu.VMEM)
-    return pl.pallas_call(
+    messages_t, forces = pl.pallas_call(
         functools.partial(kernel, 4 * rows),
-        out_shape=(jax.ShapeDtypeStruct((rows, chans), F32), jax.ShapeDtypeStruct((3, rows), F32)),
-        in_specs=[vmem] * 5,
+        out_shape=(jax.ShapeDtypeStruct((chans, rows), F32), jax.ShapeDtypeStruct((3, rows), F32)),
+        in_specs=[pl.BlockSpec(memory_space=pl.ANY)] * 5,
         out_specs=(vmem, vmem),
         scratch_shapes=[
-            pltpu.VMEM((4, 8, rows), F32),
+            pltpu.VMEM((3, rows), F32),
+            pltpu.VMEM((chans, rows), BF16),
+            pltpu.VMEM((chans, rows), BF16),
+            pltpu.VMEM((3, kn), jnp.int32),
+            pltpu.VMEM((1, chans), F32),
+            dma((5,)),
+            pltpu.VMEM((4, 3, rows), F32),
+            pltpu.VMEM((8, rows), F32),
             pltpu.VMEM((32, rows), BF16),
             pltpu.VMEM((4, 4, 128, quarter), BF16),
             pltpu.VMEM((4, 4, 2 * kn, quarter), BF16),
             pltpu.VMEM((448, 2 * kn), BF16),
             pltpu.VMEM((4, 4, 80, quarter), BF16),
             pltpu.VMEM((4, 2, 80, quarter), BF16),
-            pltpu.VMEM((4, 2, 80, quarter), BF16),
+            pltpu.VMEM((4, 80, quarter), BF16),
             pltpu.VMEM((4, 80, quarter), BF16),
             pltpu.VMEM((3, 80, quarter), BF16),
             pltpu.VMEM((3, 80, quarter), BF16),
@@ -243,7 +274,8 @@
         compiler_params=pltpu.CompilerParams(
             collective_id=0, has_side_effects=True, vmem_limit_bytes=48 * 1024 * 1024
         ),
-    )(frac, feat, cotan, kidx, smear.reshape(1, chans))
+    )(frac, feat.T, cotan.T, kidx, smear.reshape(1, chans))
+    return messages_t.T, forces
 
 
 def over_rows(table, columns):

time: 48.2 us -> 45 us (0.934)
  Pallas kernels: 44 us -> 38.8 us
  local copies, waits for them, and re-layouts: 3.34 us -> 5.24 us
    pallas_call x1, Pallas kernels: 44 us -> 38.8 us  [fast_on_device(): pl.pallas_call(functools.partial(kernel, 4 * rows), out_shape=(jax.ShapeD...]
    unnamed x11 -> x12, local copies, waits for them, and re-layouts: 2.45 us -> 5.24 us
    pallas_call x1 -> x0, local copies, waits for them, and re-layouts: 0.89 us -> none  [fast_on_device(): pl.pallas_call(functools.partial(kernel, 4 * rows), out_shape=(jax.ShapeD...]
where the time goes in v1:
time: 45 us; the launch traced here: 44.7 us
  Pallas kernels  38.8 us (86%)
  local copies, waits for them, and re-layouts  5.24 us (12%)
  between operations  0.65 us (1%)
    pallas_call x1, Pallas kernels, fast_on_device(): pl.pallas_call(functools.partial(kernel, 4 * rows), out_shape=(jax.ShapeD...  38.8 us
    unnamed x12, local copies, waits for them, and re-layouts  5.24 us

profile of v1, /device:TPU:0, one launch (start us, length us, event | category | flops | bytes accessed | tf_op | source)
XLA Modules:
  0.0 44.7 jit_solution(356773941331971142)
XLA Ops:
  0.6 0.0 copy-start.4
  0.6 0.6 %copy-done.4 = f32[64]{0:T(128)S(1)} copy-done((f32[64]{0:T(128)S(1)}, f32[64]{0:T(128)}, u32[]{:S(2)}) %copy-start.4) | copy-done | bytes 280
  1.3 0.0 copy-start
  1.3 0.9 %copy-done = bf16[1024,64]{0,1:T(8,128)(2,1)S(1)} copy-done((bf16[1024,64]{0,1:T(8,128)(2,1)S(1)}, bf16[1024,64]{0,1:T(8,128)(2,1)}, u32[]{:S(2)}) %copy-start) | copy-done | bytes 131096
  2.2 0.0 copy-start.1
  2.2 0.9 %copy-done.1 = bf16[1024,64]{0,1:T(8,128)(2,1)S(1)} copy-done((bf16[1024,64]{0,1:T(8,128)(2,1)S(1)}, bf16[1024,64]{0,1:T(8,128)(2,1)}, u32[]{:S(2)}) %copy-start.1) | copy-done | bytes 131096
  3.1 0.0 copy-start.2
  3.1 0.8 %copy-done.2 = s32[3,2048]{1,0:T(4,128)S(1)} copy-done((s32[3,2048]{1,0:T(4,128)S(1)}, s32[3,2048]{1,0:T(4,128)}, u32[]{:S(2)}) %copy-start.2) | copy-done | bytes 24600
  3.9 0.0 copy-start.3
  3.9 0.7 %copy-done.3 = f32[3,1024]{1,0:T(4,128)S(1)} copy-done((f32[3,1024]{1,0:T(4,128)S(1)}, f32[3,1024]{1,0:T(4,128)}, u32[]{:S(2)}) %copy-start.3) | copy-done | bytes 12312
  4.6 38.8 %shard_map.68 = (f32[64,1024]{1,0:T(8,128)S(1)}, f32[3,1024]{1,0:T(4,128)S(1)}) custom-call(f32[3,1024]{1,0:T(4,128)S(1)} %copy-done.3, bf16[64,1024]{1,0:T(8,128)(2,1)S(1)} %bitcast.5, bf16[64,1024]{1,0:T(8,128)(2,1)S(1)} %bitcast.6, s32[3,2048]{1,0:T(4,128)S(1)} %copy-done.2, f32[1,64]{1,0:T(1,128)S(1)} %bitcast.7), custom_call_target="tpu_custom_call" | custom-call | tf_op jit(solution)/shard_map/pallas_call | solution.py:247
  43.4 0.7 %copy.9 = f32[1024,64]{0,1:T(8,128)} copy(f32[1024,64]{0,1:T(8,128)S(1)} %bitcast.4) | data formatting | bytes 524288
  44.1 0.6 %copy.10 = f32[3,1024]{1,0:T(4,128)} copy(f32[3,1024]{1,0:T(4,128)S(1)} %get-tuple-element.9) | data formatting | bytes 24576
Async XLA Ops:
  0.6 0.7 %copy-start.4 = (f32[64]{0:T(128)S(1)}, f32[64]{0:T(128)}, u32[]{:S(2)}) copy-start(f32[64]{0:T(128)} %param.9) | copy-start | bytes 772
  1.3 0.9 %copy-start = (bf16[1024,64]{0,1:T(8,128)(2,1)S(1)}, bf16[1024,64]{0,1:T(8,128)(2,1)}, u32[]{:S(2)}) copy-start(bf16[1024,64]{0,1:T(8,128)(2,1)} %param.6) | copy-start | bytes 393220
  2.2 0.9 %copy-start.1 = (bf16[1024,64]{0,1:T(8,128)(2,1)S(1)}, bf16[1024,64]{0,1:T(8,128)(2,1)}, u32[]{:S(2)}) copy-start(bf16[1024,64]{0,1:T(8,128)(2,1)} %param.7) | copy-start | bytes 393220
  3.1 0.8 %copy-start.2 = (s32[3,2048]{1,0:T(4,128)S(1)}, s32[3,2048]{1,0:T(4,128)}, u32[]{:S(2)}) copy-start(s32[3,2048]{1,0:T(4,128)} %kidx_hbm.1) | copy-start | bytes 73732
  3.9 0.7 %copy-start.3 = (f32[3,1024]{1,0:T(4,128)S(1)}, f32[3,1024]{1,0:T(4,128)}, u32[]{:S(2)}) copy-start(f32[3,1024]{1,0:T(4,128)} %frac_hbm.1) | copy-start | bytes 36868

commit v2 on v1

--- a/solution.py
+++ b/solution.py
@@ -118,12 +118,9 @@
             ph[r, s, kn : 2 * kn, :] = sn
 
     def sums_of(r):
-        total = None
-        for s in range(4):
-            term = lax.dot_general(
-                ph[r, s], xt[r, s], (((1,), (1,)), ((), ())), preferred_element_type=F32
-            )
-            total = term if total is None else total + term
+        waves = jnp.concatenate([ph[r, s] for s in range(4)], axis=1)
+        both = jnp.concatenate([xt[r, s] for s in range(4)], axis=1)
+        total = lax.dot_general(both, waves, (((1,), (1,)), ((), ())), preferred_element_type=F32)
         return total
 
     def wait_frac(r):
@@ -156,23 +153,23 @@
     wait_frac(1)
     phases(1)
     forward_x(1)
+    total = sums_of(0)
     forward_x(3)
-    total = sums_of(0)
+    wait_frac(3)
+    phases(3)
     forward_core(1)
     forward_x(2)
-    wait_frac(3)
-    phases(3)
+    wait_frac(2)
+    phases(2)
     forward_core(3)
     wait_core(1)
     total = total + sums_of(1)
     forward_core(2)
-    wait_frac(2)
-    phases(2)
     wait_core(3)
     total = total + sums_of(3)
     wait_core(2)
     total = total + sums_of(2)
-    sums_t = total.T
+    sums_t = total
 
     wc = (sums_t[:, :kn] * weights).astype(BF16)
     ws = (sums_t[:, kn:] * weights).astype(BF16)
@@ -206,14 +203,21 @@
         c.start()
         pending.append(c)
 
-    for i in range(4):
+    def to_core(i):
         outputs_of((1 + i) % 4, i, (other_core * 2, other_core * 2 + 1))
         begin(remote(part.at[i, other_two], rc.at[i], pcs.at[i], pcr.at[i], dev_core))
-    for i in range(4):
+
+    def to_x(i):
         outputs_of((1 + i) % 4, i, (mate,))
         remote(part.at[i, two], rc.at[i], pcs.at[i], pcr.at[i], dev_core).wait_recv()
         s1[i] = (part[i, mate].astype(F32) + rc[i, 1 - x].astype(F32)).astype(BF16)
         begin(remote(s1.at[i], rx.at[i], pxs.at[i], pxr.at[i], dev_x))
+
+    to_core(0)
+    for i in range(1, 4):
+        to_core(i)
+        to_x(i - 1)
+    to_x(3)
     own = None
     for i in range(4):
         outputs_of((1 + i) % 4, i, (slot,))

time: 45 us -> 41.5 us (0.922)
  Pallas kernels: 38.8 us -> 35.3 us
    pallas_call x1, Pallas kernels: 38.8 us -> 35.3 us  [fast_on_device(): pl.pallas_call(functools.partial(kernel, 4 * rows), out_shape=(jax.ShapeD...]
where the time goes in v2:
time: 41.5 us; the launch traced here: 41.2 us
  Pallas kernels  35.3 us (85%)
  local copies, waits for them, and re-layouts  5.24 us (13%)
  between operations  0.65 us (2%)
    pallas_call x1, Pallas kernels, fast_on_device(): pl.pallas_call(functools.partial(kernel, 4 * rows), out_shape=(jax.ShapeD...  35.3 us
    unnamed x12, local copies, waits for them, and re-layouts  5.24 us

profile of v2, /device:TPU:0, one launch (start us, length us, event | category | flops | bytes accessed | tf_op | source)
XLA Modules:
  0.0 41.2 jit_solution(9003648405085296502)
XLA Ops:
  0.6 0.0 copy-start.4
  0.6 0.6 %copy-done.4 = f32[64]{0:T(128)S(1)} copy-done((f32[64]{0:T(128)S(1)}, f32[64]{0:T(128)}, u32[]{:S(2)}) %copy-start.4) | copy-done | bytes 280
  1.3 0.0 copy-start
  1.3 0.9 %copy-done = bf16[1024,64]{0,1:T(8,128)(2,1)S(1)} copy-done((bf16[1024,64]{0,1:T(8,128)(2,1)S(1)}, bf16[1024,64]{0,1:T(8,128)(2,1)}, u32[]{:S(2)}) %copy-start) | copy-done | bytes 131096
  2.2 0.0 copy-start.1
  2.2 0.9 %copy-done.1 = bf16[1024,64]{0,1:T(8,128)(2,1)S(1)} copy-done((bf16[1024,64]{0,1:T(8,128)(2,1)S(1)}, bf16[1024,64]{0,1:T(8,128)(2,1)}, u32[]{:S(2)}) %copy-start.1) | copy-done | bytes 131096
  3.1 0.0 copy-start.2
  3.1 0.8 %copy-done.2 = s32[3,2048]{1,0:T(4,128)S(1)} copy-done((s32[3,2048]{1,0:T(4,128)S(1)}, s32[3,2048]{1,0:T(4,128)}, u32[]{:S(2)}) %copy-start.2) | copy-done | bytes 24600
  3.9 0.0 copy-start.3
  3.9 0.7 %copy-done.3 = f32[3,1024]{1,0:T(4,128)S(1)} copy-done((f32[3,1024]{1,0:T(4,128)S(1)}, f32[3,1024]{1,0:T(4,128)}, u32[]{:S(2)}) %copy-start.3) | copy-done | bytes 12312
  4.6 35.3 %shard_map.68 = (f32[64,1024]{1,0:T(8,128)S(1)}, f32[3,1024]{1,0:T(4,128)S(1)}) custom-call(f32[3,1024]{1,0:T(4,128)S(1)} %copy-done.3, bf16[64,1024]{1,0:T(8,128)(2,1)S(1)} %bitcast.5, bf16[64,1024]{1,0:T(8,128)(2,1)S(1)} %bitcast.6, s32[3,2048]{1,0:T(4,128)S(1)} %copy-done.2, f32[1,64]{1,0:T(1,128)S(1)} %bitcast.7), custom_call_target="tpu_custom_call" | custom-call | tf_op jit(solution)/shard_map/pallas_call | solution.py:251
  39.9 0.7 %copy.9 = f32[1024,64]{0,1:T(8,128)} copy(f32[1024,64]{0,1:T(8,128)S(1)} %bitcast.4) | data formatting | bytes 524288
  40.6 0.6 %copy.10 = f32[3,1024]{1,0:T(4,128)} copy(f32[3,1024]{1,0:T(4,128)S(1)} %get-tuple-element.9) | data formatting | bytes 24576
Async XLA Ops:
  0.6 0.7 %copy-start.4 = (f32[64]{0:T(128)S(1)}, f32[64]{0:T(128)}, u32[]{:S(2)}) copy-start(f32[64]{0:T(128)} %param.9) | copy-start | bytes 772
  1.3 0.9 %copy-start = (bf16[1024,64]{0,1:T(8,128)(2,1)S(1)}, bf16[1024,64]{0,1:T(8,128)(2,1)}, u32[]{:S(2)}) copy-start(bf16[1024,64]{0,1:T(8,128)(2,1)} %param.6) | copy-start | bytes 393220
  2.2 0.9 %copy-start.1 = (bf16[1024,64]{0,1:T(8,128)(2,1)S(1)}, bf16[1024,64]{0,1:T(8,128)(2,1)}, u32[]{:S(2)}) copy-start(bf16[1024,64]{0,1:T(8,128)(2,1)} %param.7) | copy-start | bytes 393220
  3.1 0.8 %copy-start.2 = (s32[3,2048]{1,0:T(4,128)S(1)}, s32[3,2048]{1,0:T(4,128)}, u32[]{:S(2)}) copy-start(s32[3,2048]{1,0:T(4,128)} %kidx_hbm.1) | copy-start | bytes 73732
  3.9 0.7 %copy-start.3 = (f32[3,1024]{1,0:T(4,128)S(1)}, f32[3,1024]{1,0:T(4,128)}, u32[]{:S(2)}) copy-start(f32[3,1024]{1,0:T(4,128)} %frac_hbm.1) | copy-start | bytes 36868
